TPU v7x, 32 devices: a whole 2x2x4 slice. The times are simulated.
32 devices in a mesh: parts: 2 (over y), blk: 4 (over z), row: 2 (over x), sub: 2 (over core).
Axes of the slice: x: 2, y: 2, z: 4, core: 2. Of those that a mesh axis runs over, the one named last changes fastest.
Arguments:
- query_grads: bfloat16 [512, 4, 2048], P('blk', None, 'sub'), may hold values from -6 to 6
- curvature: bfloat16 [4, 2048, 2048], P('blk', ('row', 'sub')), may hold values from -0.125 to 0.125
- train_grads: bfloat16 [5120, 4, 2048], P(('parts', 'row', 'sub'), 'blk'), parts along dimension 0, may hold values from -0.0625 to 0.0625
- query_ids: int32 [1024], P('parts'), parts along dimension 0, may hold values from 0 to 511, each once
- block_map: int32 [4], replicated, may hold values from 0 to 3, each once
- row_ids: int32 [5120], P(('parts', 'row', 'sub')), parts along dimension 0, may hold values from 0 to 639
Outputs:
- scores: float32 [512, 5120], P('blk', ('parts', 'row', 'sub')), parts along dimension 1
There are 2 independent parts, one for each index of `parts`. A program takes and returns all parts, laid end to end along the dimension named above; an argument that names none is the same for every part. Nothing has to cross between parts.
Inputs may be any that keep to these rules, and one draw needn't show every extreme that they name: `query_ids`: each value appears once. `block_map`: each value appears once.
All inputs are finite; a program needn't handle non-finite values.
Results may differ from a plain program's by a relative error of at most 0.0029.
Values may be sent and summed in bfloat16 or wider, within the bound.
A program may use at most 64 MiB of HBM per device.

v0:
```python
import jax
import jax.numpy as jnp
from jax import lax
from jax.sharding import PartitionSpec as P


def per_device(query_grads, curvature, train_grads, query_ids, block_map, row_ids):
    mine = jnp.take(query_grads, block_map, axis=1)
    arrived = lax.all_to_all(mine, "blk", split_axis=1, concat_axis=0, tiled=True)
    queries = arrived.shape[0]
    precond = jnp.einsum(
        "qsj,sij->qsi",
        lax.all_gather(arrived, "sub", axis=2, tiled=True),
        curvature,
        preferred_element_type=jnp.float32,
    ).astype(jnp.bfloat16)
    inverse = (
        jnp.zeros((queries,), jnp.int32).at[query_ids].set(jnp.arange(queries, dtype=jnp.int32))
    )
    ordered = jnp.take(precond, inverse, axis=0)
    chosen = jnp.take(train_grads, row_ids, axis=0)
    partial_value = jnp.einsum(
        "qsk,rsk->qr",
        lax.all_gather(ordered, ("row", "sub"), axis=2, tiled=True),
        chosen,
        preferred_element_type=jnp.float32,
    )
    return lax.psum_scatter(partial_value, "blk", scatter_dimension=0, tiled=True)


def solution(mesh):
    placed = (
        P("blk", None, "sub"),
        P("blk", ("row", "sub"), None),
        P(("parts", "row", "sub"), "blk", None),
        P("parts"),
        P(),
        P(("parts", "row", "sub")),
    )
    return jax.shard_map(
        per_device,
        mesh=mesh,
        in_specs=placed,
        out_specs=P("blk", ("parts", "row", "sub")),
        check_vma=False,
    )
```

profile of v0, /device:TPU:0, one launch (start us, length us, event | category | flops | bytes accessed | tf_op | source)
XLA Modules:
  0.0 133.4 jit_solution(11992758323479835850)
XLA Ops:
  6.5 0.0 copy-start
  6.5 0.0 all-gather.3.cloned.1.call-start
  6.5 0.8 compare_and_fusion.1
  7.4 0.7 compare_select_fusion.3
  8.0 6.1 %gather_fusion = bf16[4,128,1024]{2,0,1:T(4,128)(2,1)} fusion(bf16[128,4,1024]{2,1,0:T(4,128)(2,1)} %param.6, s32[1024]{0:T(1024)S(1)} %pad_clamp_fusion.2), kind=kCustom, calls=%fused_computation | custom fusion | bytes 2097168 | tf_op jit(solution)/shard_map/jit(_take)/gather | solution.py:8
  14.1 1.7 %select_bitcast_fusion = bf16[128,4,1024]{2,1,0:T(4,128)(2,1)S(1)} fusion(bf16[4,128,1024]{2,0,1:T(4,128)(2,1)} %gather_fusion, pred[4]{0:T(512)(128)(4,1)S(1)} %compare_and_fusion.1), kind=kLoop, calls=%fused_computation.14 | loop fusion | flops 524288 | bytes 2097156 | tf_op jit(solution)/shard_map/jit(_take)/select_n | solution.py:8
  15.9 0.3 copy.8
  16.2 0.0 copy-start.2
  16.2 31.9 %all_to_all.18 = bf16[128,4,1024]{2,0,1:T(8,128)(2,1)} all-to-all(bf16[128,4,1024]{2,0,1:T(8,128)(2,1)S(1)} %copy.8), channel_id=1, replica_groups=mesh['parts'=2,'blk'=4,'row'=2,'sub'=2] {'blk'}, dimensions={1} | all-to-all | bytes 2097152 | tf_op jit(solution)/shard_map/all_to_all | solution.py:9
  48.1 0.0 all-gather.3.cloned.1.call-update
  48.2 0.0 all-gather.5.cloned.1.call-start
  48.2 0.0 copy-done.2
  48.3 2.4 %scatter_custom_fusion = s32[512]{0:T(512)S(1)} fusion(s32[512]{0:T(512)S(1)} %compare_select_fusion.2, s32[512]{0:T(512)S(1)} %iota.3, s32[]{:T(128)} %constant.30.clone.1), kind=kCustom, calls=%fused_computation.26 | custom fusion | bytes 2052 | tf_op jit(solution)/shard_map/scatter | solution.py:18
  50.7 7.3 %all-gather.3.cloned.1.call-done = bf16[512,1,2048]{2,0,1:T(8,128)(2,1)} async-done(((bf16[512,1,1024]{2,0,1:T(8,128)(2,1)}), bf16[512,1,2048]{2,0,1:T(8,128)(2,1)}) %all-gather.3.cloned.1.call-update) | async-done | bytes 2097168 | tf_op jit(solution)/shard_map/all_gather | solution.py:13
  58.0 3.5 %fusion.8 = bf16[512,512]{1,0:T(8,128)(2,1)S(1)} fusion(bf16[1,512,2048]{2,1,0:T(8,128)(2,1)} %param.7, bf16[512,1,2048]{2,0,1:T(8,128)(2,1)} %all-gather.3.cloned.1.call-done), kind=kOutput, calls=%fused_computation.13 | convolution fusion | flops 1074003968 | bytes 4718592 | tf_op jit(solution)/shard_map/qsj,sij->qsi/dot_general | solution.py:11
  61.5 0.0 copy-start.1
  61.5 2.6 %gather_fusion.1 = bf16[512,512]{1,0:T(8,128)(2,1)} fusion(bf16[512,512]{1,0:T(8,128)(2,1)S(1)} %fusion.8, s32[1024]{0:T(1024)S(1)} %pad_clamp_fusion.1), kind=kCustom, calls=%fused_computation.1 | custom fusion | bytes 1050624 | tf_op jit(solution)/shard_map/jit(_take)/gather | solution.py:20
  64.2 2.0 %bitcast_select_fusion.2 = bf16[512,1,512]{2,0,1:T(8,128)(2,1)} fusion(bf16[512,512]{1,0:T(8,128)(2,1)} %gather_fusion.1, pred[512]{0:T(512)(128)(4,1)S(1)} %compare_and_fusion.2), kind=kLoop, calls=%fused_computation.15 | loop fusion | flops 262144 | bytes 1049088 | tf_op jit(solution)/shard_map/jit(_take)/select_n | solution.py:20
  66.1 0.0 all-gather.5.cloned.1.call-update
  66.2 0.0 reduce-scatter.2.cloned.1.call-start
  66.2 0.0 copy-done.1
  66.2 0.0 copy-done
  66.3 4.1 %gather_fusion.2 = bf16[640,2048]{1,0:T(8,128)(2,1)} fusion(bf16[640,2048]{1,0:T(8,128)(2,1)S(1)} %bitcast.32, s32[1024]{0:T(1024)S(1)} %pad_clamp_fusion), kind=kCustom, calls=%fused_computation.2 | custom fusion | bytes 5245440 | tf_op jit(solution)/shard_map/jit(_take)/gather | solution.py:21
  70.3 19.7 %all-gather.5.cloned.1.call-done = bf16[512,1,2048]{2,0,1:T(8,128)(2,1)} async-done(((bf16[512,1,512]{2,0,1:T(8,128)(2,1)}), bf16[512,1,2048]{2,0,1:T(8,128)(2,1)}) %all-gather.5.cloned.1.call-update) | async-done | bytes 2097168 | tf_op jit(solution)/shard_map/all_gather | solution.py:24
  90.1 5.4 %fusion = f32[512,640]{1,0:T(8,128)} fusion(bf16[640,2048]{1,0:T(8,128)(2,1)} %gather_fusion.2, pred[640]{0:T(1024)(128)(4,1)S(1)} %compare_and_fusion, bf16[512,1,2048]{2,0,1:T(8,128)(2,1)} %all-gather.5.cloned.1.call-done), kind=kOutput, calls=%fused_computation.4 | convolution fusion | flops 1343488000 | bytes 6029952 | tf_op jit(solution)/shard_map/qsk,rsk->qr/dot_general | solution.py:22
  95.5 0.0 reduce-scatter.2.cloned.1.call-update
  95.5 31.4 %reduce-scatter.2.cloned.1.call-done = f32[128,640]{1,0:T(8,128)} async-done(((f32[512,640]{1,0:T(8,128)}), f32[128,640]{1,0:T(8,128)}) %reduce-scatter.2.cloned.1.call-update) | async-done | bytes 327696 | tf_op jit(solution)/shard_map/reduce_scatter | solution.py:28
  (9 shorter events, 0.1 us)
Async XLA Ops:
  6.5 59.7 %copy-start = (bf16[640,1,2048]{2,0,1:T(8,128)(2,1)S(1)}, bf16[640,1,2048]{2,0,1:T(8,128)(2,1)}, u32[]{:S(2)}) copy-start(bf16[640,1,2048]{2,0,1:T(8,128)(2,1)} %param.8) | copy-start | bytes 7864324
  6.5 51.5 %all-gather.3.cloned.1.call-start = ((), (), s32[]{:S(2)}) async-start(), calls=%async_computation.2 | async-start | bytes 3145728 | tf_op jit(solution)/shard_map/all_gather | solution.py:13
  16.2 32.0 %copy-start.2 = (s32[512]{0:T(512)S(1)}, s32[512]{0:T(512)}, u32[]{:S(2)}) copy-start(s32[512]{0:T(512)} %param.9) | copy-start | bytes 6148
  48.2 41.9 %all-gather.5.cloned.1.call-start = ((), (), s32[]{:S(2)}) async-start(), calls=%async_computation.3 | async-start | bytes 2621440 | tf_op jit(solution)/shard_map/all_gather | solution.py:24
  61.5 4.7 %copy-start.1 = (s32[640]{0:T(1024)S(1)}, s32[640]{0:T(1024)}, u32[]{:S(2)}) copy-start(s32[640]{0:T(1024)} %param.11) | copy-start | bytes 7684
  66.2 60.7 %reduce-scatter.2.cloned.1.call-start = ((), (), s32[]{:S(2)}) async-start(), calls=%async_computation.4 | async-start | bytes 1638400 | tf_op jit(solution)/shard_map/reduce_scatter | solution.py:28
Sparse Core Ops, SparseCore 0:
  48.3 9.6 all-gather.2
  66.3 23.7 all-gather.4
  95.6 31.2 reduce-scatter.1
where the time goes:
time: 134 us; the launch traced here: 133 us
  waiting for transfers between devices  58.4 us (44%)
  blocking collectives  31.9 us (24%)
  local copies, waits for them, and re-layouts  15.6 us (12%)
  between operations  13.2 us (10%)
  matrix products  8.88 us (7%)
  other arithmetic  5.23 us (4%)
    all_to_all x1, blocking collectives, per_device(): lax.all_to_all(mine, 'blk', split_axis=1, concat_axis=0, tiled=True)  31.9 us
    reduce_scatter x1, waiting for transfers between devices, per_device(): lax.psum_scatter(partial_value, 'blk', scatter_dimension=0, tiled=True)  31.4 us
    all_gather x1, waiting for transfers between devices, per_device(): lax.all_gather(ordered, ('row', 'sub'), axis=2, tiled=True)  19.7 us
    all_gather x1, waiting for transfers between devices, per_device(): lax.all_gather(arrived, 'sub', axis=2, tiled=True)  7.28 us
    gather x1, local copies, waits for them, and re-layouts, per_device(): mine = jnp.take(query_grads, block_map, axis=1)  6.11 us
    dot_general x1, matrix products, per_device(): jnp.einsum('qsk,rsk->qr', lax.all_gather(ordered, ('row', 'sub'), axis=2,...  5.39 us
    gather x1, local copies, waits for them, and re-layouts, per_device(): chosen = jnp.take(train_grads, row_ids, axis=0)  4.06 us
    dot_general x1, matrix products, per_device(): jnp.einsum('qsj,sij->qsi', lax.all_gather(arrived, 'sub', axis=2, tiled=T...  3.5 us
  transfers between devices with their start and end apart: 3, of which 3 were waited for; matrix products, arithmetic and copies ran while one was open for 5% of the time, Pallas kernels for 0%

commit v1 on v0

v1 whole, which is shorter than its diff:
```python
import functools

import jax
import jax.numpy as jnp
from jax import lax
from jax.experimental import pallas as pl
from jax.experimental.pallas import tpu as pltpu
from jax.sharding import PartitionSpec as P

MESH = pl.DeviceIdType.MESH
F32 = jnp.float32
BF16 = jnp.bfloat16
NT = (((1,), (1,)), ((), ()))
TN = (((0,), (0,)), ((), ()))


def aligned(index, size):
    return pl.ds(pl.multiple_of(index * size, size), size)


def kernel(
    nb, nx, names,
    block_map, query_ids, row_ids, q_hbm, curv_hbm, train_hbm, out_ref,
    q_ref, curv, train, chosen, stage, grouped, precond, mine, sent, arrived,
    load_sem, z_send, z_recv, a_send, a_recv, c_send, c_recv, e_send, e_recv,
):
    p, b, r, s = (lax.axis_index(name) for name in ("parts", "blk", "row", "sub"))
    rows = q_ref.shape[0]
    half = q_ref.shape[1] // nb
    piece = half // (2 * nx)
    own_cols = curv.shape[0]
    part_cols = own_cols // 2

    def at(parts=None, blk=None, row=None, sub=None):
        return (
            p if parts is None else parts,
            b if blk is None else blk,
            r if row is None else row,
            s if sub is None else sub,
        )

    loads = [
        pltpu.make_async_copy(q_hbm, q_ref, load_sem.at[0]),
        pltpu.make_async_copy(train_hbm, train, load_sem.at[1]),
        pltpu.make_async_copy(curv_hbm, curv, load_sem.at[2]),
    ]
    for load in loads:
        load.start()

    other = 1 - s
    mate = 1 - p
    peers = [lax.rem(r + o, nx) for o in range(nx)]
    origins = [lax.rem(r + nx - o, nx) for o in range(nx)]
    sources = [lax.rem(b + d, nb) for d in range(nb)]

    barrier = pltpu.get_barrier_semaphore()
    everyone = [at(blk=sources[d]) for d in range(1, nb)]
    everyone += [at(row=peers[o]) for o in range(1, nx)]
    everyone += [at(parts=mate), at(sub=other)]
    for device in everyone:
        pl.semaphore_signal(barrier, inc=1, device_id=device, device_id_type=MESH)

    loads[0].wait()
    for d in range(nb):
        target = lax.rem(b + nb - d, nb)

        def add(block, total, slot=block_map[target]):
            weight = jnp.where(slot == block, 1.0, 0.0)
            values = q_ref[:, aligned(block * 2 * nx + p * nx + r, piece)]
            return total + weight * values.astype(F32)

        zeros = jnp.zeros((rows, piece), F32)
        block = lax.fori_loop(0, nb, add, zeros, unroll=nb <= 8).astype(BF16)
        if d:
            stage[d] = block
        else:
            grouped[aligned(b, rows), aligned(s * 2 * nx + p * nx + r, piece)] = block
    pl.semaphore_wait(barrier, len(everyone))

    started = []

    def remote(ref_from, ref_to, send, recv, device):
        return pltpu.make_async_remote_copy(
            src_ref=ref_from, dst_ref=ref_to, send_sem=send, recv_sem=recv,
            device_id=device, device_id_type=MESH,
        )

    def go(*args):
        copy = remote(*args)
        copy.start()
        started.append(copy)

    def arrive(ref, send, recv):
        remote(ref, ref, send, recv, at(sub=other)).wait_recv()

    def spot(d, parts, row):
        return grouped.at[aligned(sources[d], rows), aligned(s * 2 * nx + parts * nx + row, piece)]

    def half_spot(d, sub):
        return grouped.at[aligned(sources[d], rows), aligned(sub, half)]

    def p_spot(d, row, sub):
        return precond.at[aligned(sources[d], rows), aligned(row * 2 + sub, own_cols)]

    def p_half(d, row, sub, parts):
        return precond.at[
            aligned(sources[d], rows), aligned((row * 2 + sub) * 2 + parts, part_cols)
        ]

    for d in range(1, nb):
        go(stage.at[d], spot(0, p, r), z_send.at[d], z_recv.at[d], at(blk=lax.rem(b + nb - d, nb)))

    def spread(d):
        if d:
            arrive(spot(d, p, r), z_send.at[d], z_recv.at[d])
        for o in range(1, nx):
            go(spot(d, p, r), spot(d, p, r), a_send.at[d, o], a_recv.at[d, o], at(row=peers[o]))
        go(spot(d, p, r), spot(d, p, r), a_send.at[d, nx], a_recv.at[d, nx], at(parts=mate))

    def second(d):
        for o in range(1, nx):
            arrive(spot(d, p, origins[o]), a_send.at[d, o], a_recv.at[d, o])
            if d % 2 == 0:
                place = spot(d, p, origins[o])
                go(place, place, a_send.at[d, nx + o], a_recv.at[d, nx + o], at(parts=mate))
        arrive(spot(d, mate, r), a_send.at[d, nx], a_recv.at[d, nx])
        if d % 2 == 1:
            place = spot(d, mate, r)
            for o in range(1, nx):
                go(place, place, a_send.at[d, nx + o], a_recv.at[d, nx + o], at(row=peers[o]))

    def across(d):
        for o in range(1, nx):
            arrive(spot(d, mate, origins[o]), a_send.at[d, nx + o], a_recv.at[d, nx + o])
        place = half_spot(d, s)
        go(place, place, a_send.at[d, 2 * nx], a_recv.at[d, 2 * nx], at(sub=other))

    def apply(d):
        arrive(half_spot(d, other), a_send.at[d, 2 * nx], a_recv.at[d, 2 * nx])
        result = lax.dot_general(
            grouped[aligned(sources[d], rows), :], curv[...], NT, preferred_element_type=F32
        )
        precond[aligned(sources[d], rows), aligned(r * 2 + s, own_cols)] = result.astype(BF16)
        place = p_half(d, r, s, p)
        for o in range(1, nx):
            go(place, place, c_send.at[d, o], c_recv.at[d, o], at(row=peers[o]))
        place = p_spot(d, r, s)
        go(place, place, c_send.at[d, 0], c_recv.at[d, 0], at(sub=other))

    def forward(d):
        for o in range(1, nx):
            place = p_half(d, origins[o], s, p)
            arrive(place, c_send.at[d, o], c_recv.at[d, o])
            go(place, place, c_send.at[d, nx + o], c_recv.at[d, nx + o], at(parts=mate))

    def share(d):
        for o in range(1, nx):
            arrive(p_half(d, origins[o], s, mate), c_send.at[d, nx + o], c_recv.at[d, nx + o])
            place = p_spot(d, origins[o], s)
            go(place, place, c_send.at[d, 2 * nx + o], c_recv.at[d, 2 * nx + o], at(sub=other))

    def finish(d):
        arrive(p_spot(d, r, other), c_send.at[d, 0], c_recv.at[d, 0])
        for o in range(1, nx):
            arrive(p_spot(d, origins[o], other), c_send.at[d, 2 * nx + o], c_recv.at[d, 2 * nx + o])

    def choose():
        loads[1].wait()
        count = train.shape[0]
        pick = (lax.broadcasted_iota(jnp.int32, (count, count), 0) == row_ids[...])
        pick = jnp.where(pick, 1.0, 0.0).astype(BF16)
        width = 512

        @pl.loop(0, train.shape[1] // width)
        def _(step):
            chosen[:, aligned(step, width)] = lax.dot_general(
                pick, train[:, aligned(step, width)], TN, preferred_element_type=F32
            ).astype(BF16)

    steps = [spread, second, across, apply, forward, share, finish]
    for t in range(nb + len(steps) - 1):
        for lag, step in enumerate(steps):
            if 0 <= t - lag < nb:
                step(t - lag)
        if t == 0:
            choose()
            loads[2].wait()

    def score(target):
        outs = lax.broadcasted_iota(jnp.int32, (rows, precond.shape[0]), 0) + target * rows
        pick = jnp.where(outs == query_ids[...], 1.0, 0.0).astype(BF16)
        ordered = jnp.dot(pick, precond[...], preferred_element_type=F32).astype(BF16)
        return lax.dot_general(ordered, chosen[...], NT, preferred_element_type=F32)

    def exchange(e):
        target = lax.rem(b + e, nb)
        return remote(sent.at[e], arrived.at[e], e_send.at[e], e_recv.at[e], at(blk=target))

    @pl.loop(1, nb)
    def _(e):
        sent[e] = score(lax.rem(b + e, nb)).astype(BF16)
        exchange(e).start()

    mine[...] = score(b)
    for copy in started:
        copy.wait_send()

    @pl.loop(1, nb)
    def _(e):
        exchange(e).wait()
        mine[...] += arrived[e].astype(F32)

    out_ref[...] = mine[...]


def per_device(nb, nx, names, query_grads, curvature, train_grads, query_ids, block_map, row_ids):
    rows, blocks, half = query_grads.shape
    queries = query_ids.shape[0]
    features = curvature.shape[2]
    count = train_grads.shape[0]
    smem = pl.BlockSpec(memory_space=pltpu.SMEM)
    vmem = pl.BlockSpec(memory_space=pltpu.VMEM)
    hbm = pl.BlockSpec(memory_space=pl.ANY)
    dma = pltpu.SemaphoreType.DMA
    return pl.pallas_call(
        functools.partial(kernel, nb, nx, names),
        out_shape=jax.ShapeDtypeStruct((rows, count), F32),
        in_specs=[smem, vmem, vmem, hbm, hbm, hbm],
        out_specs=vmem,
        scratch_shapes=[
            pltpu.VMEM((rows, blocks * half), BF16),
            pltpu.VMEM(curvature.shape[1:], BF16),
            pltpu.VMEM((count, features), BF16),
            pltpu.VMEM((count, features), BF16),
            pltpu.VMEM((nb, rows, half // (2 * nx)), BF16),
            pltpu.VMEM((queries, features), BF16),
            pltpu.VMEM((queries, features), BF16),
            pltpu.VMEM((rows, count), F32),
            pltpu.VMEM((nb, rows, count), BF16),
            pltpu.VMEM((nb, rows, count), BF16),
            dma((3,)),
            dma((nb,)),
            dma((nb,)),
            dma((nb, 2 * nx + 1)),
            dma((nb, 2 * nx + 1)),
            dma((nb, 3 * nx)),
            dma((nb, 3 * nx)),
            dma((nb,)),
            dma((nb,)),
        ],
        compiler_params=pltpu.CompilerParams(
            collective_id=0, has_side_effects=True, vmem_limit_bytes=63 * 2**20
        ),
        cost_estimate=pl.CostEstimate(
            flops=2 * queries * features * (curvature.shape[1] + count),
            bytes_accessed=8 * 2**20,
            transcendentals=0,
        ),
    )(
        block_map,
        query_ids.reshape(1, queries),
        row_ids.reshape(1, count),
        query_grads.reshape(rows, blocks * half),
        curvature.reshape(curvature.shape[1:]),
        train_grads.reshape(count, features),
    )


def solution(mesh):
    placed = (
        P("blk", None, "sub"),
        P("blk", ("row", "sub"), None),
        P(("parts", "row", "sub"), "blk", None),
        P("parts"),
        P(),
        P(("parts", "row", "sub")),
    )
    return jax.shard_map(
        functools.partial(per_device, mesh.shape["blk"], mesh.shape["row"], mesh.axis_names),
        mesh=mesh,
        in_specs=placed,
        out_specs=P("blk", ("parts", "row", "sub")),
        check_vma=False,
    )
```

time: 134 us -> 56.6 us (0.42)
  the two profiles are of different devices: /device:TPU:0 before, /device:TPU:9 now
where the time goes in v1:
time: 56.6 us; the launch traced here: 56.4 us
  Pallas kernels  50.8 us (90%)
  local copies, waits for them, and re-layouts  5.57 us (10%)
    pallas_call x1, Pallas kernels, per_device(): pl.pallas_call(functools.partial(kernel, nb, nx, names), out_shape=jax.Sh...  50.8 us
    unnamed x2, local copies, waits for them, and re-layouts  4.31 us
    reshape x1, local copies, waits for them, and re-layouts, per_device(): row_ids.reshape(1, count)  1.27 us

profile of v1, /device:TPU:9, one launch (start us, length us, event | category | flops | bytes accessed | tf_op | source)
XLA Modules:
  0.0 56.4 jit_solution(1239941308355432272)
XLA Ops:
  0.0 1.3 %reshape.16.row_ids = s32[1,640]{1,0:T(1,128)} reshape(s32[640]{0:T(1024)} %param.11) | data formatting | bytes 5120 | tf_op jit(solution)/shard_map/reshape | solution.py:262
  1.3 2.6 %copy.7 = bf16[16,8,4,1024]{3,1,2,0:T(8,128)(2,1)} copy(bf16[16,8,4,1024]{3,2,1,0:T(4,128)(2,1)} %bitcast.5) | data formatting | bytes 2097152
  3.9 50.8 %shard_map.64 = f32[128,640]{1,0:T(8,128)} custom-call(s32[4]{0:T(128)} %block_map.1, s32[1,512]{1,0:T(1,128)} %bitcast.9, s32[1,640]{1,0:T(1,128)} %reshape.16.row_ids, bf16[128,4096]{1,0:T(8,128)(2,1)} %bitcast.6, bf16[512,2048]{1,0:T(8,128)(2,1)} %bitcast.8, bf16[640,2048]{1,0:T(8,128)(2,1)} %bitcast.7), custom_call_target="tpu_custom_call" | custom-call | flops 2415919104 | bytes 8388608 | tf_op jit(solution)/shard_map/pallas_call | solution.py:225
  54.7 1.7 %copy.9 = f32[128,640]{1,0:T(8,128)} copy(f32[128,640]{1,0:T(8,128)} %shard_map.64) | data formatting | bytes 655360

commit v2 on v1

--- a/solution.py
+++ b/solution.py
@@ -11,7 +11,6 @@
 F32 = jnp.float32
 BF16 = jnp.bfloat16
 NT = (((1,), (1,)), ((), ()))
-TN = (((0,), (0,)), ((), ()))
 
 
 def aligned(index, size):
@@ -21,15 +20,14 @@
 def kernel(
     nb, nx, names,
     block_map, query_ids, row_ids, q_hbm, curv_hbm, train_hbm, out_ref,
-    q_ref, curv, train, chosen, stage, grouped, precond, mine, sent, arrived,
+    q_ref, curv, train, chosen, row_pick, stage, grouped, precond, mine, sent, arrived,
     load_sem, z_send, z_recv, a_send, a_recv, c_send, c_recv, e_send, e_recv,
 ):
     p, b, r, s = (lax.axis_index(name) for name in ("parts", "blk", "row", "sub"))
     rows = q_ref.shape[0]
-    half = q_ref.shape[1] // nb
-    piece = half // (2 * nx)
+    piece = q_ref.shape[1] // nb
+    half = 2 * nx * piece
     own_cols = curv.shape[0]
-    part_cols = own_cols // 2
 
     def at(parts=None, blk=None, row=None, sub=None):
         return (
@@ -66,8 +64,7 @@
 
         def add(block, total, slot=block_map[target]):
             weight = jnp.where(slot == block, 1.0, 0.0)
-            values = q_ref[:, aligned(block * 2 * nx + p * nx + r, piece)]
-            return total + weight * values.astype(F32)
+            return total + weight * q_ref[:, aligned(block, piece)].astype(F32)
 
         zeros = jnp.zeros((rows, piece), F32)
         block = lax.fori_loop(0, nb, add, zeros, unroll=nb <= 8).astype(BF16)
@@ -99,13 +96,8 @@
     def half_spot(d, sub):
         return grouped.at[aligned(sources[d], rows), aligned(sub, half)]
 
-    def p_spot(d, row, sub):
-        return precond.at[aligned(sources[d], rows), aligned(row * 2 + sub, own_cols)]
-
-    def p_half(d, row, sub, parts):
-        return precond.at[
-            aligned(sources[d], rows), aligned((row * 2 + sub) * 2 + parts, part_cols)
-        ]
+    def p_spot(e, row, sub):
+        return precond.at[aligned(sources[e], rows), aligned(row * 2 + sub, own_cols)]
 
     for d in range(1, nb):
         go(stage.at[d], spot(0, p, r), z_send.at[d], z_recv.at[d], at(blk=lax.rem(b + nb - d, nb)))
@@ -135,73 +127,70 @@
         place = half_spot(d, s)
         go(place, place, a_send.at[d, 2 * nx], a_recv.at[d, 2 * nx], at(sub=other))
 
-    def apply(d):
+    def settle(d):
         arrive(half_spot(d, other), a_send.at[d, 2 * nx], a_recv.at[d, 2 * nx])
+
+    count = train.shape[0]
+    width = train.shape[1] // nb
+
+    def choose(d):
+        if d == 0:
+            loads[1].wait()
+            pick = lax.broadcasted_iota(jnp.int32, (count, count), 0) == row_ids[...].reshape(1, count)
+            row_pick[...] = jnp.where(pick, 1.0, 0.0).astype(BF16).T
+        if width % 128 == 0 or d == 0:
+            cols = pl.ds(d * width, width) if width % 128 == 0 else pl.ds(0, train.shape[1])
+            chosen[:, cols] = jnp.dot(
+                row_pick[...], train[:, cols], preferred_element_type=F32
+            ).astype(BF16)
+
+    def pipeline(steps, count):
+        for t in range(count + max(lag for lag, _ in steps)):
+            for lag, step in steps:
+                if 0 <= t - lag < count:
+                    step(t - lag)
+
+    pipeline([(0, spread), (1, second), (0, choose), (2, across), (3, settle)], nb)
+    loads[2].wait()
+
+    def apply(e):
+        outs = lax.broadcasted_iota(jnp.int32, (rows, grouped.shape[0]), 0) + sources[e] * rows
+        pick = jnp.where(outs == query_ids[...], 1.0, 0.0).astype(BF16)
+        ordered = jnp.dot(pick, grouped[...], preferred_element_type=F32).astype(BF16)
+        result = lax.dot_general(ordered, curv[...], NT, preferred_element_type=F32)
+        precond[aligned(sources[e], rows), aligned(r * 2 + s, own_cols)] = result.astype(BF16)
+        place = p_spot(e, r, s)
+        for o in range(1, nx):
+            go(place, place, c_send.at[e, o], c_recv.at[e, o], at(row=peers[o]))
+        go(place, place, c_send.at[e, 0], c_recv.at[e, 0], at(sub=other))
+
+    def share(e):
+        for o in range(1, nx):
+            place = p_spot(e, origins[o], s)
+            arrive(place, c_send.at[e, o], c_recv.at[e, o])
+            go(place, place, c_send.at[e, nx + o], c_recv.at[e, nx + o], at(sub=other))
+
+    def score(e):
+        arrive(p_spot(e, r, other), c_send.at[e, 0], c_recv.at[e, 0])
+        for o in range(1, nx):
+            arrive(p_spot(e, origins[o], other), c_send.at[e, nx + o], c_recv.at[e, nx + o])
         result = lax.dot_general(
-            grouped[aligned(sources[d], rows), :], curv[...], NT, preferred_element_type=F32
+            precond[aligned(sources[e], rows), :], chosen[...], NT, preferred_element_type=F32
         )
-        precond[aligned(sources[d], rows), aligned(r * 2 + s, own_cols)] = result.astype(BF16)
-        place = p_half(d, r, s, p)
-        for o in range(1, nx):
-            go(place, place, c_send.at[d, o], c_recv.at[d, o], at(row=peers[o]))
-        place = p_spot(d, r, s)
-        go(place, place, c_send.at[d, 0], c_recv.at[d, 0], at(sub=other))
-
-    def forward(d):
-        for o in range(1, nx):
-            place = p_half(d, origins[o], s, p)
-            arrive(place, c_send.at[d, o], c_recv.at[d, o])
-            go(place, place, c_send.at[d, nx + o], c_recv.at[d, nx + o], at(parts=mate))
-
-    def share(d):
-        for o in range(1, nx):
-            arrive(p_half(d, origins[o], s, mate), c_send.at[d, nx + o], c_recv.at[d, nx + o])
-            place = p_spot(d, origins[o], s)
-            go(place, place, c_send.at[d, 2 * nx + o], c_recv.at[d, 2 * nx + o], at(sub=other))
-
-    def finish(d):
-        arrive(p_spot(d, r, other), c_send.at[d, 0], c_recv.at[d, 0])
-        for o in range(1, nx):
-            arrive(p_spot(d, origins[o], other), c_send.at[d, 2 * nx + o], c_recv.at[d, 2 * nx + o])
-
-    def choose():
-        loads[1].wait()
-        count = train.shape[0]
-        pick = (lax.broadcasted_iota(jnp.int32, (count, count), 0) == row_ids[...])
-        pick = jnp.where(pick, 1.0, 0.0).astype(BF16)
-        width = 512
-
-        @pl.loop(0, train.shape[1] // width)
-        def _(step):
-            chosen[:, aligned(step, width)] = lax.dot_general(
-                pick, train[:, aligned(step, width)], TN, preferred_element_type=F32
-            ).astype(BF16)
-
-    steps = [spread, second, across, apply, forward, share, finish]
-    for t in range(nb + len(steps) - 1):
-        for lag, step in enumerate(steps):
-            if 0 <= t - lag < nb:
-                step(t - lag)
-        if t == 0:
-            choose()
-            loads[2].wait()
-
-    def score(target):
-        outs = lax.broadcasted_iota(jnp.int32, (rows, precond.shape[0]), 0) + target * rows
-        pick = jnp.where(outs == query_ids[...], 1.0, 0.0).astype(BF16)
-        ordered = jnp.dot(pick, precond[...], preferred_element_type=F32).astype(BF16)
-        return lax.dot_general(ordered, chosen[...], NT, preferred_element_type=F32)
+        if e:
+            sent[e] = result.astype(BF16)
+            exchange(e).start()
+        else:
+            mine[...] = result
 
     def exchange(e):
         target = lax.rem(b + e, nb)
         return remote(sent.at[e], arrived.at[e], e_send.at[e], e_recv.at[e], at(blk=target))
 
-    @pl.loop(1, nb)
-    def _(e):
-        sent[e] = score(lax.rem(b + e, nb)).astype(BF16)
-        exchange(e).start()
-
-    mine[...] = score(b)
+    def turn(step):
+        return lambda t: step((t + 1) % nb)
+
+    pipeline([(0, turn(apply)), (2, turn(score)), (1, turn(share))], nb)
     for copy in started:
         copy.wait_send()
 
@@ -218,6 +207,9 @@
     queries = query_ids.shape[0]
     features = curvature.shape[2]
     count = train_grads.shape[0]
+    piece = half // (2 * nx)
+    spot = lax.axis_index("parts") * nx + lax.axis_index("row")
+    part = lax.dynamic_slice_in_dim(query_grads, spot * piece, piece, axis=2)
     smem = pl.BlockSpec(memory_space=pltpu.SMEM)
     vmem = pl.BlockSpec(memory_space=pltpu.VMEM)
     hbm = pl.BlockSpec(memory_space=pl.ANY)
@@ -228,11 +220,12 @@
         in_specs=[smem, vmem, vmem, hbm, hbm, hbm],
         out_specs=vmem,
         scratch_shapes=[
-            pltpu.VMEM((rows, blocks * half), BF16),
+            pltpu.VMEM((rows, blocks * piece), BF16),
             pltpu.VMEM(curvature.shape[1:], BF16),
             pltpu.VMEM((count, features), BF16),
             pltpu.VMEM((count, features), BF16),
-            pltpu.VMEM((nb, rows, half // (2 * nx)), BF16),
+            pltpu.VMEM((count, count), BF16),
+            pltpu.VMEM((nb, rows, piece), BF16),
             pltpu.VMEM((queries, features), BF16),
             pltpu.VMEM((queries, features), BF16),
             pltpu.VMEM((rows, count), F32),
@@ -243,13 +236,13 @@
             dma((nb,)),
             dma((nb, 2 * nx + 1)),
             dma((nb, 2 * nx + 1)),
-            dma((nb, 3 * nx)),
-            dma((nb, 3 * nx)),
+            dma((nb, 2 * nx)),
+            dma((nb, 2 * nx)),
             dma((nb,)),
             dma((nb,)),
         ],
         compiler_params=pltpu.CompilerParams(
-            collective_id=0, has_side_effects=True, vmem_limit_bytes=63 * 2**20
+            collective_id=0, has_side_effects=True, vmem_limit_bytes=62 * 2**20
         ),
         cost_estimate=pl.CostEstimate(
             flops=2 * queries * features * (curvature.shape[1] + count),
@@ -259,8 +252,8 @@
     )(
         block_map,
         query_ids.reshape(1, queries),
-        row_ids.reshape(1, count),
-        query_grads.reshape(rows, blocks * half),
+        row_ids,
+        part.reshape(rows, blocks * piece),
         curvature.reshape(curvature.shape[1:]),
         train_grads.reshape(count, features),
     )

time: 56.6 us -> 52.7 us (0.931)
  Pallas kernels: 50.8 us -> 48.7 us
  local copies, waits for them, and re-layouts: 5.57 us -> 3.78 us
    pallas_call x1, Pallas kernels: 50.8 us -> 48.7 us  [per_device(): pl.pallas_call(functools.partial(kernel, nb, nx, names), out_shape=jax.Sh...]
    reshape x1 -> x0, local copies, waits for them, and re-layouts: 1.27 us -> none  [per_device(): row_ids.reshape(1, count)]
    unnamed x2 -> x4, local copies, waits for them, and re-layouts: 4.31 us -> 3.68 us
where the time goes in v2:
time: 52.7 us; the launch traced here: 52.5 us
  Pallas kernels  48.7 us (92%)
  local copies, waits for them, and re-layouts  3.78 us (7%)
    pallas_call x1, Pallas kernels, per_device(): pl.pallas_call(functools.partial(kernel, nb, nx, names), out_shape=jax.Sh...  48.7 us
    unnamed x4, local copies, waits for them, and re-layouts  3.68 us

profile of v2, /device:TPU:9, one launch (start us, length us, event | category | flops | bytes accessed | tf_op | source)
XLA Modules:
  0.0 52.5 jit_solution(5087264043647250162)
XLA Ops:
  0.0 0.0 copy-start
  0.0 1.2 %copy-done = bf16[128,4,1024]{2,1,0:T(4,128)(2,1)S(1)} copy-done((bf16[128,4,1024]{2,1,0:T(4,128)(2,1)S(1)}, bf16[128,4,1024]{2,1,0:T(4,128)(2,1)}, u32[]{:S(2)}) %copy-start) | copy-done | bytes 1048600
  1.2 0.1 constant_dynamic-slice_fusion
  1.3 0.7 %copy.7 = bf16[16,8,4,256]{3,1,2,0:T(8,128)(2,1)} copy(bf16[16,8,4,256]{3,2,1,0:T(4,128)(2,1)S(1)} %bitcast.5) | data formatting | bytes 524288
  2.1 48.7 %shard_map.64 = f32[128,640]{1,0:T(8,128)} custom-call(s32[4]{0:T(128)} %block_map.1, s32[1,512]{1,0:T(1,128)} %bitcast.9, s32[640]{0:T(1024)} %row_ids.1, bf16[128,1024]{1,0:T(8,128)(2,1)} %bitcast.6, bf16[512,2048]{1,0:T(8,128)(2,1)} %bitcast.8, bf16[640,2048]{1,0:T(8,128)(2,1)} %bitcast.7), custom_call_target="tpu_custom_call" | custom-call | flops 2415919104 | bytes 8388608 | tf_op jit(solution)/shard_map/pallas_call | solution.py:217
  50.7 1.7 %copy.9 = f32[128,640]{1,0:T(8,128)} copy(f32[128,640]{1,0:T(8,128)} %shard_map.64) | data formatting | bytes 655360
Async XLA Ops:
  0.0 1.2 %copy-start = (bf16[128,4,1024]{2,1,0:T(4,128)(2,1)S(1)}, bf16[128,4,1024]{2,1,0:T(4,128)(2,1)}, u32[]{:S(2)}) copy-start(bf16[128,4,1024]{2,1,0:T(4,128)(2,1)} %param.6) | copy-start | bytes 3145732

commit v3 on v2

--- a/solution.py
+++ b/solution.py
@@ -187,8 +187,10 @@
         target = lax.rem(b + e, nb)
         return remote(sent.at[e], arrived.at[e], e_send.at[e], e_recv.at[e], at(blk=target))
 
+    order = sorted(range(1, nb), key=lambda e: abs(2 * e - nb)) + [0]
+
     def turn(step):
-        return lambda t: step((t + 1) % nb)
+        return lambda t: step(order[t])
 
     pipeline([(0, turn(apply)), (2, turn(score)), (1, turn(share))], nb)
     for copy in started:

time: 52.7 us -> 50.8 us (0.964); the launches traced: 52.5 us -> 49.9 us
  Pallas kernels: 48.7 us -> 46.2 us
    pallas_call x1, Pallas kernels: 48.7 us -> 46.2 us  [per_device(): pl.pallas_call(functools.partial(kernel, nb, nx, names), out_shape=jax.Sh...]
where the time goes in v3:
time: 50.8 us; the launch traced here: 49.9 us
  Pallas kernels  46.2 us (91%)
  local copies, waits for them, and re-layouts  3.78 us (7%)
    pallas_call x1, Pallas kernels, per_device(): pl.pallas_call(functools.partial(kernel, nb, nx, names), out_shape=jax.Sh...  46.2 us
    unnamed x4, local copies, waits for them, and re-layouts  3.68 us

profile of v3, /device:TPU:9, one launch (start us, length us, event | category | flops | bytes accessed | tf_op | source)
XLA Modules:
  0.0 49.9 jit_solution(12259907129708837970)
XLA Ops:
  0.0 0.0 copy-start
  0.0 1.2 %copy-done = bf16[128,4,1024]{2,1,0:T(4,128)(2,1)S(1)} copy-done((bf16[128,4,1024]{2,1,0:T(4,128)(2,1)S(1)}, bf16[128,4,1024]{2,1,0:T(4,128)(2,1)}, u32[]{:S(2)}) %copy-start) | copy-done | bytes 1048600
  1.2 0.1 constant_dynamic-slice_fusion
  1.3 0.7 %copy.7 = bf16[16,8,4,256]{3,1,2,0:T(8,128)(2,1)} copy(bf16[16,8,4,256]{3,2,1,0:T(4,128)(2,1)S(1)} %bitcast.5) | data formatting | bytes 524288
  2.1 46.2 %shard_map.64 = f32[128,640]{1,0:T(8,128)} custom-call(s32[4]{0:T(128)} %block_map.1, s32[1,512]{1,0:T(1,128)} %bitcast.9, s32[640]{0:T(1024)} %row_ids.1, bf16[128,1024]{1,0:T(8,128)(2,1)} %bitcast.6, bf16[512,2048]{1,0:T(8,128)(2,1)} %bitcast.8, bf16[640,2048]{1,0:T(8,128)(2,1)} %bitcast.7), custom_call_target="tpu_custom_call" | custom-call | flops 2415919104 | bytes 8388608 | tf_op jit(solution)/shard_map/pallas_call | solution.py:219
  48.2 1.7 %copy.9 = f32[128,640]{1,0:T(8,128)} copy(f32[128,640]{1,0:T(8,128)} %shard_map.64) | data formatting | bytes 655360
Async XLA Ops:
  0.0 1.2 %copy-start = (bf16[128,4,1024]{2,1,0:T(4,128)(2,1)S(1)}, bf16[128,4,1024]{2,1,0:T(4,128)(2,1)}, u32[]{:S(2)}) copy-start(bf16[128,4,1024]{2,1,0:T(4,128)(2,1)} %param.6) | copy-start | bytes 3145732

commit v4 on v3

--- a/solution.py
+++ b/solution.py
@@ -19,7 +19,7 @@
 
 def kernel(
     nb, nx, names,
-    block_map, query_ids, row_ids, q_hbm, curv_hbm, train_hbm, out_ref,
+    block_map, query_ids, row_ids, q_hbm, curv_hbm, train_hbm, out_ref, last_ref,
     q_ref, curv, train, chosen, row_pick, stage, grouped, precond, mine, sent, arrived,
     load_sem, z_send, z_recv, a_send, a_recv, c_send, c_recv, e_send, e_recv,
 ):
@@ -196,12 +196,14 @@
     for copy in started:
         copy.wait_send()
 
-    @pl.loop(1, nb)
+    @pl.loop(1, nb - 1)
     def _(e):
         exchange(e).wait()
         mine[...] += arrived[e].astype(F32)
 
     out_ref[...] = mine[...]
+    exchange(nb - 1).wait()
+    last_ref[...] = arrived[nb - 1]
 
 
 def per_device(nb, nx, names, query_grads, curvature, train_grads, query_ids, block_map, row_ids):
@@ -216,11 +218,11 @@
     vmem = pl.BlockSpec(memory_space=pltpu.VMEM)
     hbm = pl.BlockSpec(memory_space=pl.ANY)
     dma = pltpu.SemaphoreType.DMA
-    return pl.pallas_call(
+    total, last = pl.pallas_call(
         functools.partial(kernel, nb, nx, names),
-        out_shape=jax.ShapeDtypeStruct((rows, count), F32),
+        out_shape=[jax.ShapeDtypeStruct((rows, count), kind) for kind in (F32, BF16)],
         in_specs=[smem, vmem, vmem, hbm, hbm, hbm],
-        out_specs=vmem,
+        out_specs=[vmem, vmem],
         scratch_shapes=[
             pltpu.VMEM((rows, blocks * piece), BF16),
             pltpu.VMEM(curvature.shape[1:], BF16),
@@ -259,6 +261,7 @@
         curvature.reshape(curvature.shape[1:]),
         train_grads.reshape(count, features),
     )
+    return total + last.astype(F32)
 
 
 def solution(mesh):

time: 50.8 us -> 50.9 us (level)
  other arithmetic: 0 us -> 1.77 us
  local copies, waits for them, and re-layouts: 3.78 us -> 2.06 us
    add x0 -> x1, other arithmetic: none -> 1.77 us  [per_device(): return total + last.astype(F32)]
    unnamed x4 -> x3, local copies, waits for them, and re-layouts: 3.68 us -> 1.96 us
where the time goes in v4:
time: 50.9 us; the launch traced here: 50 us
  Pallas kernels  46.2 us (91%)
  local copies, waits for them, and re-layouts  2.06 us (4%)
  other arithmetic  1.77 us (3%)
    pallas_call x1, Pallas kernels, per_device(): pl.pallas_call(functools.partial(kernel, nb, nx, names), out_shape=[jax.S...  46.2 us
    unnamed x3, local copies, waits for them, and re-layouts  1.96 us
    add x1, other arithmetic, per_device(): return total + last.astype(F32)  1.77 us

profile of v4, /device:TPU:9, one launch (start us, length us, event | category | flops | bytes accessed | tf_op | source)
XLA Modules:
  0.0 50.0 jit_solution(11235390146470045162)
XLA Ops:
  0.0 0.0 copy-start
  0.0 1.2 %copy-done = bf16[128,4,1024]{2,1,0:T(4,128)(2,1)S(1)} copy-done((bf16[128,4,1024]{2,1,0:T(4,128)(2,1)S(1)}, bf16[128,4,1024]{2,1,0:T(4,128)(2,1)}, u32[]{:S(2)}) %copy-start) | copy-done | bytes 1048600
  1.2 0.1 constant_dynamic-slice_fusion
  1.3 0.7 %copy.7 = bf16[16,8,4,256]{3,1,2,0:T(8,128)(2,1)} copy(bf16[16,8,4,256]{3,2,1,0:T(4,128)(2,1)S(1)} %bitcast.5) | data formatting | bytes 524288
  2.1 46.2 %shard_map.64 = (f32[128,640]{1,0:T(8,128)}, bf16[128,640]{1,0:T(8,128)(2,1)}) custom-call(s32[4]{0:T(128)} %block_map.1, s32[1,512]{1,0:T(1,128)} %bitcast.9, s32[640]{0:T(1024)} %row_ids.1, bf16[128,1024]{1,0:T(8,128)(2,1)} %bitcast.6, bf16[512,2048]{1,0:T(8,128)(2,1)} %bitcast.8, bf16[640,2048]{1,0:T(8,128)(2,1)} %bitcast.7), custom_call_target="tpu_custom_call" | custom-call | flops 2415919104 | bytes 8388608 | tf_op jit(solution)/shard_map/pallas_call | solution.py:221
  48.3 1.8 %convert_add_fusion = f32[128,640]{1,0:T(8,128)} fusion(f32[128,640]{1,0:T(8,128)} %get-tuple-element.7, bf16[128,640]{1,0:T(8,128)(2,1)} %get-tuple-element.8), kind=kLoop, calls=%fused_computation | loop fusion | flops 163840 | bytes 819200 | tf_op jit(solution)/shard_map/add | solution.py:264
Async XLA Ops:
  0.0 1.2 %copy-start = (bf16[128,4,1024]{2,1,0:T(4,128)(2,1)S(1)}, bf16[128,4,1024]{2,1,0:T(4,128)(2,1)}, u32[]{:S(2)}) copy-start(bf16[128,4,1024]{2,1,0:T(4,128)(2,1)} %param.6) | copy-start | bytes 3145732
